TPU v7x, 512 devices: a whole 4x4x16 slice. The times are simulated.
512 devices in a mesh: pipe: 32 (over z_lo, x), tensor: 16 (over z_hi, y, core).
Axes of the slice: x: 4, y: 4, z: 16 (z_hi: 2, z_lo: 8; z = z_hi * 8 + z_lo), core: 2. Of those that a mesh axis runs over, the one named last changes fastest.
Arguments:
- in_flight: bfloat16 [4, 4096, 7168], P(None, 'pipe', 'tensor'), may hold values from -6 to 6
- entering: bfloat16 [4, 2, 128, 7168], P(None, None, None, 'tensor'), may hold values from -6 to 6
- saved_inputs: bfloat16 [2, 2, 4096, 7168], P(None, None, 'pipe', 'tensor'), may hold values from -6 to 6
- latent_down: bfloat16 [32, 7168, 512], P('pipe', 'tensor'), may hold values from -1 to 1
- latent_back: bfloat16 [32, 512, 7168], P('pipe', None, 'tensor'), may hold values from -0.25 to 0.25
Outputs:
- section_outputs: bfloat16 [2, 2, 4096, 7168], P(None, None, 'pipe', 'tensor')
- input_grads: bfloat16 [2, 2, 4096, 7168], P(None, None, 'pipe', 'tensor')
- grad_down: bfloat16 [32, 7168, 512], P('pipe', 'tensor')
- grad_back: bfloat16 [32, 512, 7168], P('pipe', None, 'tensor')
All inputs are finite; a program needn't handle non-finite values.
Results may differ from a plain program's by a relative error of at most 0.012.
Values may be sent and summed in bfloat16 or wider, within the bound.
A program may use at most 64 MiB of HBM per device.

v0:
```python
import jax
import jax.numpy as jnp
from jax import lax
from jax.sharding import PartitionSpec as P

D = 7168
LAT = 512
STEPS = 2


eps = 1e-06


def swapped(block, axis, bit):
    count = lax.axis_size(axis)
    route = []
    for low in range(count):
        high = low | 1 << bit
        if high != low and high < count:
            route += [(low, high), (high, low)]
    return lax.ppermute(block, axis, route)


def from_behind(value, axis, steps):
    count = lax.axis_size(axis)
    initial, last = (max(0, -steps), min(count, count - steps))
    return lax.ppermute(value, axis, [(source, source + steps) for source in range(initial, last)])


def flip_order(count):
    return list(range(count))


def mirror_weights(values, count):
    for level in flip_order(count):
        values = swapped(values, "pipe", level)
    return values


def mirror_gradients(values, count):
    for level in flip_order(count):
        values = swapped(values, "pipe", level)
    return values


def attend(latent):
    scores = jnp.einsum("stl,sul->stu", latent, latent, preferred_element_type=jnp.float32) * (
        4.0 / LAT
    )
    rows = lax.broadcasted_iota(jnp.int32, scores.shape, 1)
    cols = lax.broadcasted_iota(jnp.int32, scores.shape, 2)
    scores = jnp.where(rows >= cols, scores, -jnp.inf)
    probs = jax.nn.softmax(scores, axis=2)
    probs_b = probs.astype(jnp.bfloat16)
    mixed = jnp.einsum("stu,sul->stl", probs_b, latent, preferred_element_type=jnp.float32).astype(
        jnp.bfloat16
    )
    return (probs, probs_b, mixed)


def layers(east_in, west_in, east_kept, west_kept, east_cot, west_cot, downs, backs):
    inputs = jnp.stack([east_in, west_in, east_kept, west_kept])
    weights = jnp.concatenate([downs, downs], axis=0)
    raw = jnp.einsum("sti,sil->stl", inputs, weights, preferred_element_type=jnp.float32)
    wide = inputs.astype(jnp.float32)
    squares = jnp.sum(wide * wide, axis=2)
    raw, squares = lax.psum((raw, squares), "tensor")
    rscale = lax.rsqrt(squares / D + eps)
    latent = (raw * rscale[..., None]).astype(jnp.bfloat16)
    probs, probs_b, mixed = attend(latent)
    outputs = (
        wide[:2] + jnp.einsum("stl,sli->sti", mixed[:2], backs, preferred_element_type=jnp.float32)
    ).astype(jnp.bfloat16)
    cotangent = jnp.stack([east_cot, west_cot])
    grad_back = jnp.einsum("stl,sti->sli", mixed[2:], cotangent, preferred_element_type=jnp.float32)
    dmixed = jnp.einsum("sti,sli->stl", cotangent, backs, preferred_element_type=jnp.float32)
    dmixed = lax.psum(dmixed, "tensor").astype(jnp.bfloat16)
    latent_kept = latent[2:]
    probs_kept = probs[2:]
    dprobs = jnp.einsum("stl,sul->stu", dmixed, latent_kept, preferred_element_type=jnp.float32)
    dscores = probs_kept * (dprobs - jnp.sum(probs_kept * dprobs, axis=2, keepdims=True))
    dsym = ((dscores + jnp.swapaxes(dscores, 1, 2)) * (4.0 / LAT)).astype(jnp.bfloat16)
    dlatent = jnp.einsum("stu,sul->stl", dsym, latent_kept, preferred_element_type=jnp.float32)
    dlatent = dlatent + jnp.einsum(
        "sut,sul->stl", probs_b[2:], dmixed, preferred_element_type=jnp.float32
    )
    scale_kept = rscale[2:]
    draw = (dlatent * scale_kept[..., None]).astype(jnp.bfloat16)
    grad_down = jnp.einsum("sti,stl->sil", inputs[2:], draw, preferred_element_type=jnp.float32)
    dscale = jnp.sum(dlatent * raw[2:], axis=2)
    result = cotangent.astype(jnp.float32) + jnp.einsum(
        "stl,sil->sti", draw, downs, preferred_element_type=jnp.float32
    )
    result = result - wide[2:] * (scale_kept * scale_kept * scale_kept * dscale / D)[..., None]
    result = result.astype(jnp.bfloat16)
    return (outputs[0], outputs[1], result[0], result[1], grad_down, grad_back)


def combine(first, second):
    first_b, second_b = lax.optimization_barrier((first.astype(jnp.bfloat16), second))
    return (first_b.astype(jnp.float32) + second_b.astype(jnp.float32)).astype(jnp.bfloat16)


def shards(in_flight, entering, saved_inputs, latent_down, latent_back):
    depth = lax.axis_size("pipe")
    levels = depth.bit_length() - 1
    position = lax.axis_index("pipe")
    at_first = position == 0
    at_last = position == depth - 1
    own_down = latent_down[0]
    own_back = latent_back[0]
    local = own_down.shape[0]
    width = own_down.shape[1]
    packed = jnp.concatenate([own_down.reshape(-1), own_back.reshape(-1)])
    packed = mirror_weights(packed, levels)
    far_down = packed[: local * width].reshape(local, width)
    far_back = packed[local * width :].reshape(width, local)
    downs = jnp.stack([own_down, far_down])
    backs = jnp.stack([own_back, far_back])
    east_act = in_flight[0]
    west_act = in_flight[1]
    east_grad = in_flight[2]
    west_grad = in_flight[3]
    sum_down = jnp.zeros((2, local, width), jnp.float32)
    sum_back = jnp.zeros((2, width, local), jnp.float32)
    outs_east, outs_west, grads_east, grads_west = ([], [], [], [])
    for step in range(STEPS):
        moving_right = from_behind(jnp.stack([east_act, west_grad]), "pipe", 1)
        moving_left = from_behind(jnp.stack([west_act, east_grad]), "pipe", -1)
        east_in = jnp.where(at_first, entering[0, step], moving_right[0])
        west_cot = jnp.where(at_first, entering[3, step], moving_right[1])
        west_in = jnp.where(at_last, entering[1, step], moving_left[0])
        east_cot = jnp.where(at_last, entering[2, step], moving_left[1])
        east_act, west_act, east_grad, west_grad, part_down, part_back = layers(
            east_in,
            west_in,
            saved_inputs[0, step],
            saved_inputs[1, step],
            east_cot,
            west_cot,
            downs,
            backs,
        )
        sum_down = sum_down + part_down
        sum_back = sum_back + part_back
        outs_east.append(east_act)
        outs_west.append(west_act)
        grads_east.append(east_grad)
        grads_west.append(west_grad)
    west_part = jnp.concatenate(
        [sum_down[1].astype(jnp.bfloat16).reshape(-1), sum_back[1].astype(jnp.bfloat16).reshape(-1)]
    )
    west_part = mirror_gradients(west_part, levels)
    west_down = west_part[: local * width].reshape(local, width)
    west_back = west_part[local * width :].reshape(width, local)
    grad_down = combine(sum_down[0], west_down)
    grad_back = combine(sum_back[0], west_back)
    section_outputs = jnp.stack([jnp.stack(outs_east), jnp.stack(outs_west)])
    input_grads = jnp.stack([jnp.stack(grads_east), jnp.stack(grads_west)])
    return (section_outputs, input_grads, grad_down[None], grad_back[None])


def solution(mesh):
    in_specs = (
        P(None, "pipe", "tensor"),
        P(None, None, None, "tensor"),
        P(None, None, "pipe", "tensor"),
        P("pipe", "tensor", None),
        P("pipe", None, "tensor"),
    )
    out_specs = (
        P(None, None, "pipe", "tensor"),
        P(None, None, "pipe", "tensor"),
        P("pipe", "tensor", None),
        P("pipe", None, "tensor"),
    )
    return jax.shard_map(shards, mesh=mesh, in_specs=in_specs, out_specs=out_specs, check_vma=False)
```

profile of v0, /device:TPU:25, one launch (start us, length us, event | category | flops | bytes accessed | tf_op | source)
XLA Modules:
  0.0 1000.9 jit_solution(7725509812601390293)
XLA Ops:
  9.4 3.1 collective-permute-start.2
  12.5 20.0 %collective-permute-done.2 = bf16[458752]{0:T(1024)(128)(2,1)S(1)} collective-permute-done((bf16[458752]{0:T(1024)(128)(2,1)S(1)}, bf16[458752]{0:T(1024)(128)(2,1)S(1)}, u32[]{:S(2)}, u32[]{:S(2)}) %collective-permute-start.2) | collective-permute-done | bytes 917536 | tf_op jit(solution)/shard_map/ppermute | solution.py:21
  32.5 4.6 collective-permute-start.3
  37.1 19.0 %collective-permute-done.3 = bf16[458752]{0:T(1024)(128)(2,1)S(1)} collective-permute-done((bf16[458752]{0:T(1024)(128)(2,1)S(1)}, bf16[458752]{0:T(1024)(128)(2,1)S(1)}, u32[]{:S(2)}, u32[]{:S(2)}) %collective-permute-start.3) | collective-permute-done | bytes 917536 | tf_op jit(solution)/shard_map/ppermute | solution.py:21
  56.2 3.5 collective-permute-start.4
  59.7 18.1 %collective-permute-done.4 = bf16[458752]{0:T(1024)(128)(2,1)S(1)} collective-permute-done((bf16[458752]{0:T(1024)(128)(2,1)S(1)}, bf16[458752]{0:T(1024)(128)(2,1)S(1)}, u32[]{:S(2)}, u32[]{:S(2)}) %collective-permute-start.4) | collective-permute-done | bytes 917536 | tf_op jit(solution)/shard_map/ppermute | solution.py:21
  77.8 4.9 collective-permute-start.5
  83.4 1.3 collective-permute-start.1
  84.7 37.5 %collective-permute-done.5 = bf16[458752]{0:T(1024)(128)(2,1)} collective-permute-done((bf16[458752]{0:T(1024)(128)(2,1)S(1)}, bf16[458752]{0:T(1024)(128)(2,1)}, u32[]{:S(2)}, u32[]{:S(2)}) %collective-permute-start.5) | collective-permute-done | bytes 917536 | tf_op jit(solution)/shard_map/ppermute | solution.py:21
  122.2 8.8 collective-permute-start.6
  131.7 3.8 collective-permute-start
  135.6 1.8 slice_bitcast_fusion.4
  138.1 2.0 slice_select_fusion.5
  140.1 69.8 %collective-permute-done.6 = bf16[458752]{0:T(1024)(128)(2,1)} collective-permute-done((bf16[458752]{0:T(1024)(128)(2,1)}, bf16[458752]{0:T(1024)(128)(2,1)}, u32[]{:S(2)}, u32[]{:S(2)}) %collective-permute-start.6) | collective-permute-done | bytes 917536 | tf_op jit(solution)/shard_map/ppermute | solution.py:21
  209.9 2.1 fusion.73
  212.1 2.1 slice.229
  215.4 1.5 fusion.70
  219.4 1.5 slice.232
  221.9 1.7 fusion.47
  223.6 131.2 %all-reduce.10 = (f32[4,128]{1,0:T(4,128)S(1)}, bf16[2,128,512]{2,1,0:T(8,128)(2,1)}) all-reduce(f32[4,128]{1,0:T(4,128)S(1)} %copy-done.50, f32[2,128,512]{2,1,0:T(8,128)S(1)} %fusion.47), channel_id=1, replica_groups=mesh['pipe'=32,'tensor'=16] {'tensor'}, use_global_device_ids=true, to_apply=%region_2.3 | all-reduce | flops 131584 | bytes 790528 | tf_op jit(solution)/shard_map/psum | solution.py:67
  354.8 129.8 %all-reduce.7.cloned.1.call-done = f32[4,128,512]{2,1,0:T(8,128)} async-done(((f32[4,128,512]{2,1,0:T(8,128)}), f32[4,128,512]{2,1,0:T(8,128)}) %all-reduce.7.cloned.1.call-update) | async-done | bytes 1048592 | tf_op jit(solution)/shard_map/psum | solution.py:67
  484.6 1.4 multiply_convert_fusion.1
  490.6 1.7 copy.27
  492.3 1.3 fusion.25
  493.6 1.4 fusion.15
  495.9 1.3 collective-permute-start.8
  497.3 4.0 collective-permute-start.7
  501.3 2.6 collective-permute-done.8
  503.9 1.8 collective-permute-done.7
  507.1 1.5 fusion.68
  508.6 1.4 fusion.31
  510.0 1.6 fusion.46
  511.8 130.9 %all-reduce.11 = (f32[4,128]{1,0:T(4,128)S(1)}, bf16[2,128,512]{2,1,0:T(8,128)(2,1)}) all-reduce(f32[4,128]{1,0:T(4,128)S(1)} %multiply_reduce_fusion, f32[2,128,512]{2,1,0:T(8,128)S(1)} %fusion.46), channel_id=1, replica_groups=mesh['pipe'=32,'tensor'=16] {'tensor'}, use_global_device_ids=true, to_apply=%region_10.11 | all-reduce | flops 131584 | bytes 790528 | tf_op jit(solution)/shard_map/psum | solution.py:67
  642.7 134.7 %all-reduce.9.cloned.1.call-done = f32[4,128,512]{2,1,0:T(8,128)} async-done(((f32[4,128,512]{2,1,0:T(8,128)}), f32[4,128,512]{2,1,0:T(8,128)}) %all-reduce.9.cloned.1.call-update) | async-done | bytes 1048592 | tf_op jit(solution)/shard_map/psum | solution.py:67
  777.4 1.4 multiply_convert_fusion
  783.2 1.7 copy.32
  784.9 1.3 fusion.21
  786.2 1.5 fusion.14
  791.9 3.2 collective-permute-start.9
  795.1 19.6 %collective-permute-done.9 = bf16[458752]{0:T(1024)(128)(2,1)S(1)} collective-permute-done((bf16[458752]{0:T(1024)(128)(2,1)S(1)}, bf16[458752]{0:T(1024)(128)(2,1)S(1)}, u32[]{:S(2)}, u32[]{:S(2)}) %collective-permute-start.9) | collective-permute-done | bytes 917536 | tf_op jit(solution)/shard_map/ppermute | solution.py:21
  814.6 4.5 collective-permute-start.10
  819.1 20.8 %collective-permute-done.10 = bf16[458752]{0:T(1024)(128)(2,1)S(1)} collective-permute-done((bf16[458752]{0:T(1024)(128)(2,1)S(1)}, bf16[458752]{0:T(1024)(128)(2,1)S(1)}, u32[]{:S(2)}, u32[]{:S(2)}) %collective-permute-start.10) | collective-permute-done | bytes 917536 | tf_op jit(solution)/shard_map/ppermute | solution.py:21
  840.0 1.9 collective-permute-start.11
  841.9 21.5 %collective-permute-done.11 = bf16[458752]{0:T(1024)(128)(2,1)S(1)} collective-permute-done((bf16[458752]{0:T(1024)(128)(2,1)S(1)}, bf16[458752]{0:T(1024)(128)(2,1)S(1)}, u32[]{:S(2)}, u32[]{:S(2)}) %collective-permute-start.11) | collective-permute-done | bytes 917536 | tf_op jit(solution)/shard_map/ppermute | solution.py:21
  863.4 1.9 collective-permute-start.12
  865.9 42.1 %collective-permute-done.12 = bf16[458752]{0:T(1024)(128)(2,1)S(1)} collective-permute-done((bf16[458752]{0:T(1024)(128)(2,1)S(1)}, bf16[458752]{0:T(1024)(128)(2,1)S(1)}, u32[]{:S(2)}, u32[]{:S(2)}) %collective-permute-start.12) | collective-permute-done | bytes 917536 | tf_op jit(solution)/shard_map/ppermute | solution.py:21
  908.0 1.9 collective-permute-start.13
  912.2 79.0 %collective-permute-done.13 = bf16[458752]{0:T(1024)(128)(2,1)S(1)} collective-permute-done((bf16[458752]{0:T(1024)(128)(2,1)S(1)}, bf16[458752]{0:T(1024)(128)(2,1)S(1)}, u32[]{:S(2)}, u32[]{:S(2)}) %collective-permute-start.13) | collective-permute-done | bytes 917536 | tf_op jit(solution)/shard_map/ppermute | solution.py:21
  (170 shorter events, 30.1 us)
Async XLA Ops:
  7.2 1.9 copy-start
  7.2 477.4 %all-reduce.7.cloned.1.call-start = ((), (), s32[]{:S(2)}) async-start(), calls=%async_computation | async-start | bytes 2097152 | tf_op jit(solution)/shard_map/psum | solution.py:67
  8.5 74.2 %copy-start.44 = (bf16[4,128,448]{1,2,0:T(8,128)(2,1)S(1)}, bf16[4,128,448]{1,2,0:T(8,128)(2,1)}, u32[]{:S(2)}) copy-start(bf16[4,128,448]{1,2,0:T(8,128)(2,1)} %param.5) | copy-start | bytes 1376260
  9.4 23.1 %collective-permute-start.2 = (bf16[458752]{0:T(1024)(128)(2,1)S(1)}, bf16[458752]{0:T(1024)(128)(2,1)S(1)}, u32[]{:S(2)}, u32[]{:S(2)}) collective-permute-start(bf16[458752]{0:T(1024)(128)(2,1)S(1)} %pad_maximum_fusion), channel_id=1, source_target_pairs={{0,16},{16,0},{32,48},{48,32},{64,80},{80,64},{96,112},{112,96},{1... | collective-permute-start | bytes 2752520 | tf_op jit(solution)/shard_map/ppermute | solution.py:21
  32.5 23.7 %collective-permute-start.3 = (bf16[458752]{0:T(1024)(128)(2,1)S(1)}, bf16[458752]{0:T(1024)(128)(2,1)S(1)}, u32[]{:S(2)}, u32[]{:S(2)}) collective-permute-start(bf16[458752]{0:T(1024)(128)(2,1)S(1)} %collective-permute-done.2), channel_id=1, source_target_pairs={{0,32},{32,0},{16,48},{48,16},{64,96},{96,64},{80,112},{112,80},{1... | collective-permute-start | bytes 2752520 | tf_op jit(solution)/shard_map/ppermute | solution.py:21
  56.2 21.6 %collective-permute-start.4 = (bf16[458752]{0:T(1024)(128)(2,1)S(1)}, bf16[458752]{0:T(1024)(128)(2,1)S(1)}, u32[]{:S(2)}, u32[]{:S(2)}) collective-permute-start(bf16[458752]{0:T(1024)(128)(2,1)S(1)} %collective-permute-done.3), channel_id=1, source_target_pairs={{0,64},{64,0},{16,80},{80,16},{32,96},{96,32},{48,112},{112,48},{1... | collective-permute-start | bytes 2752520 | tf_op jit(solution)/shard_map/ppermute | solution.py:21
  77.8 44.4 %collective-permute-start.5 = (bf16[458752]{0:T(1024)(128)(2,1)S(1)}, bf16[458752]{0:T(1024)(128)(2,1)}, u32[]{:S(2)}, u32[]{:S(2)}) collective-permute-start(bf16[458752]{0:T(1024)(128)(2,1)S(1)} %collective-permute-done.4), channel_id=1, source_target_pairs={{0,128},{128,0},{16,144},{144,16},{32,160},{160,32},{48,176},{176,... | collective-permute-start | bytes 2752520 | tf_op jit(solution)/shard_map/ppermute | solution.py:21
  83.4 54.0 %collective-permute-start.1 = (bf16[2,128,448]{1,2,0:T(8,128)(2,1)}, bf16[2,128,448]{1,2,0:T(8,128)(2,1)}, u32[]{:S(2)}, u32[]{:S(2)}) collective-permute-start(bf16[2,128,448]{1,2,0:T(8,128)(2,1)} %stack.73), channel_id=1, source_target_pairs={{16,0},{32,16},{48,32},{64,48},{80,64},{96,80},{112,96},{128,112},... | collective-permute-start | bytes 688136 | tf_op jit(solution)/shard_map/ppermute | solution.py:27
  122.2 87.7 %collective-permute-start.6 = (bf16[458752]{0:T(1024)(128)(2,1)}, bf16[458752]{0:T(1024)(128)(2,1)}, u32[]{:S(2)}, u32[]{:S(2)}) collective-permute-start(bf16[458752]{0:T(1024)(128)(2,1)} %collective-permute-done.5), channel_id=1, source_target_pairs={{0,256},{256,0},{16,272},{272,16},{32,288},{288,32},{48,304},{304,... | collective-permute-start | bytes 2752520 | tf_op jit(solution)/shard_map/ppermute | solution.py:21
  131.7 6.4 collective-permute-start
  137.4 81.0 %copy-start.8 = (bf16[1,128,448]{1,2,0:T(8,128)(2,1)}, bf16[1,128,448]{1,2,0:T(8,128)(2,1)S(1)}, u32[]{:S(2)}) copy-start(bf16[1,128,448]{1,2,0:T(8,128)(2,1)S(1)} %get-tuple-element.41) | copy-start | bytes 344068
  137.4 81.0 %copy-start.9 = (bf16[1,128,448]{1,2,0:T(8,128)(2,1)}, bf16[1,128,448]{1,2,0:T(8,128)(2,1)S(1)}, u32[]{:S(2)}) copy-start(bf16[1,128,448]{1,2,0:T(8,128)(2,1)S(1)} %get-tuple-element.42) | copy-start | bytes 344068
  215.4 2.4 copy-start.19
  216.9 560.5 %all-reduce.9.cloned.1.call-start = ((), (), s32[]{:S(2)}) async-start(), calls=%async_computation.1 | async-start | bytes 2097152 | tf_op jit(solution)/shard_map/psum | solution.py:67
  219.4 4.1 copy-start.50
  221.9 264.1 %copy-start.49 = (pred[4,128,128]{1,2,0:T(32,128)(4,1)S(1)}, pred[4,128,128]{1,2,0:T(32,128)(4,1)}, u32[]{:S(2)}) copy-start(pred[4,128,128]{1,2,0:T(32,128)(4,1)} %copy.23) | copy-start | bytes 196612
  492.2 2.8 copy-start.11
  492.2 2.8 copy-start.36
  492.3 2.8 copy-start.38
  495.0 2.2 copy-start.28
  495.1 10.6 %copy-start.43 = (bf16[4,2,128,448]{2,3,1,0:T(8,128)(2,1)S(1)}, bf16[4,2,128,448]{2,3,1,0:T(8,128)(2,1)}, u32[]{:S(2)}) copy-start(bf16[4,2,128,448]{2,3,1,0:T(8,128)(2,1)} %param.6) | copy-start | bytes 2752516
  495.6 11.5 %copy-start.2 = (bf16[1,128,448]{1,2,0:T(8,128)(2,1)S(1)}, bf16[1,128,448]{1,2,0:T(8,128)(2,1)}, u32[]{:S(2)}) copy-start(bf16[1,128,448]{1,2,0:T(8,128)(2,1)} %get-tuple-element.40) | copy-start | bytes 344068
  495.6 11.5 %copy-start.5 = (bf16[1,128,448]{1,2,0:T(8,128)(2,1)S(1)}, bf16[1,128,448]{1,2,0:T(8,128)(2,1)}, u32[]{:S(2)}) copy-start(bf16[1,128,448]{1,2,0:T(8,128)(2,1)} %get-tuple-element.43) | copy-start | bytes 344068
  495.6 8.2 copy-start.32
  495.6 8.2 copy-start.34
  495.9 7.9 collective-permute-start.8
  497.3 8.4 collective-permute-start.7
  508.6 3.1 copy-start.13
  508.6 3.1 copy-start.16
  779.9 2.2 copy-start.27
  784.9 2.8 copy-start.3
  784.9 2.8 copy-start.6
  790.9 74.4 %copy-start.4 = (bf16[1,128,448]{1,2,0:T(8,128)(2,1)S(1)}, bf16[1,128,448]{1,2,0:T(8,128)(2,1)}, u32[]{:S(2)}) copy-start(bf16[1,128,448]{1,2,0:T(8,128)(2,1)} %get-tuple-element.40) | copy-start | bytes 344068
  790.9 74.4 %copy-start.7 = (bf16[1,128,448]{1,2,0:T(8,128)(2,1)S(1)}, bf16[1,128,448]{1,2,0:T(8,128)(2,1)}, u32[]{:S(2)}) copy-start(bf16[1,128,448]{1,2,0:T(8,128)(2,1)} %get-tuple-element.43) | copy-start | bytes 344068
  791.0 74.4 %copy-start.14 = (bf16[1,128,448]{1,2,0:T(8,128)(2,1)S(1)}, bf16[1,128,448]{1,2,0:T(8,128)(2,1)}, u32[]{:S(2)}) copy-start(bf16[1,128,448]{1,2,0:T(8,128)(2,1)} %copy-done.12) | copy-start | bytes 344068
  791.0 74.4 %copy-start.17 = (bf16[1,128,448]{1,2,0:T(8,128)(2,1)S(1)}, bf16[1,128,448]{1,2,0:T(8,128)(2,1)}, u32[]{:S(2)}) copy-start(bf16[1,128,448]{1,2,0:T(8,128)(2,1)} %copy-done.15) | copy-start | bytes 344068
  791.7 73.7 %copy-start.25 = (bf16[4,128,512]{2,1,0:T(8,128)(2,1)S(1)}, bf16[4,128,512]{2,1,0:T(8,128)(2,1)}, u32[]{:S(2)}) copy-start(bf16[4,128,512]{2,1,0:T(8,128)(2,1)} %convolution_convert_fusion) | copy-start | bytes 1572868
  791.8 73.7 %copy-start.46 = (bf16[1,512,448]{1,2,0:T(8,128)(2,1)S(1)}, bf16[1,512,448]{1,2,0:T(8,128)(2,1)}, u32[]{:S(2)}) copy-start(bf16[1,512,448]{1,2,0:T(8,128)(2,1)} %param.9) | copy-start | bytes 1376260
  791.8 73.7 %copy-start.48 = (bf16[1,512,448]{1,2,0:T(8,128)(2,1)S(1)}, bf16[1,512,448]{1,2,0:T(8,128)(2,1)}, u32[]{:S(2)}) copy-start(bf16[1,512,448]{1,2,0:T(8,128)(2,1)} %copy.26) | copy-start | bytes 1376260
  791.9 22.8 %collective-permute-start.9 = (bf16[458752]{0:T(1024)(128)(2,1)S(1)}, bf16[458752]{0:T(1024)(128)(2,1)S(1)}, u32[]{:S(2)}, u32[]{:S(2)}) collective-permute-start(bf16[458752]{0:T(1024)(128)(2,1)S(1)} %pad_maximum_fusion.2), channel_id=1, source_target_pairs={{0,16},{16,0},{32,48},{48,32},{64,80},{80,64},{96,112},{112,96},{1... | collective-permute-start | bytes 2752520 | tf_op jit(solution)/shard_map/ppermute | solution.py:21
  814.6 25.3 %collective-permute-start.10 = (bf16[458752]{0:T(1024)(128)(2,1)S(1)}, bf16[458752]{0:T(1024)(128)(2,1)S(1)}, u32[]{:S(2)}, u32[]{:S(2)}) collective-permute-start(bf16[458752]{0:T(1024)(128)(2,1)S(1)} %collective-permute-done.9), channel_id=1, source_target_pairs={{0,32},{32,0},{16,48},{48,16},{64,96},{96,64},{80,112},{112,80},{1... | collective-permute-start | bytes 2752520 | tf_op jit(solution)/shard_map/ppermute | solution.py:21
  840.0 23.4 %collective-permute-start.11 = (bf16[458752]{0:T(1024)(128)(2,1)S(1)}, bf16[458752]{0:T(1024)(128)(2,1)S(1)}, u32[]{:S(2)}, u32[]{:S(2)}) collective-permute-start(bf16[458752]{0:T(1024)(128)(2,1)S(1)} %collective-permute-done.10), channel_id=1, source_target_pairs={{0,64},{64,0},{16,80},{80,16},{32,96},{96,32},{48,112},{112,48},{1... | collective-permute-start | bytes 2752520 | tf_op jit(solution)/shard_map/ppermute | solution.py:21
  863.4 44.7 %collective-permute-start.12 = (bf16[458752]{0:T(1024)(128)(2,1)S(1)}, bf16[458752]{0:T(1024)(128)(2,1)S(1)}, u32[]{:S(2)}, u32[]{:S(2)}) collective-permute-start(bf16[458752]{0:T(1024)(128)(2,1)S(1)} %collective-permute-done.11), channel_id=1, source_target_pairs={{0,128},{128,0},{16,144},{144,16},{32,160},{160,32},{48,176},{176,... | collective-permute-start | bytes 2752520 | tf_op jit(solution)/shard_map/ppermute | solution.py:21
  865.5 44.5 %copy-start.29 = (bf16[1,128,448]{1,2,0:T(8,128)(2,1)S(1)}, bf16[1,128,448]{1,2,0:T(8,128)(2,1)}, u32[]{:S(2)}) copy-start(bf16[1,128,448]{1,2,0:T(8,128)(2,1)} %get-tuple-element.52) | copy-start | bytes 344068
  865.5 44.5 %copy-start.31 = (bf16[1,128,448]{1,2,0:T(8,128)(2,1)S(1)}, bf16[1,128,448]{1,2,0:T(8,128)(2,1)}, u32[]{:S(2)}) copy-start(bf16[1,128,448]{1,2,0:T(8,128)(2,1)} %get-tuple-element.53) | copy-start | bytes 344068
  865.5 45.4 %copy-start.42 = (bf16[1,128,448]{1,2,0:T(8,128)(2,1)S(1)}, bf16[1,128,448]{1,2,0:T(8,128)(2,1)}, u32[]{:S(2)}) copy-start(bf16[1,128,448]{1,2,0:T(8,128)(2,1)} %get-tuple-element.31) | copy-start | bytes 344068
  908.0 83.2 %collective-permute-start.13 = (bf16[458752]{0:T(1024)(128)(2,1)S(1)}, bf16[458752]{0:T(1024)(128)(2,1)S(1)}, u32[]{:S(2)}, u32[]{:S(2)}) collective-permute-start(bf16[458752]{0:T(1024)(128)(2,1)S(1)} %collective-permute-done.12), channel_id=1, source_target_pairs={{0,256},{256,0},{16,272},{272,16},{32,288},{288,32},{48,304},{304,... | collective-permute-start | bytes 2752520 | tf_op jit(solution)/shard_map/ppermute | solution.py:21
  991.6 1.6 copy-start.21
  (19 other events, 23.2 us)
Sparse Core Ops, SparseCore 0:
  217.0 267.5 all-reduce.6
  508.7 268.6 all-reduce.8
where the time goes:
time: 1000 us
  waiting for transfers between devices  617 us (62%)
  blocking collectives  262 us (26%)
  starting transfers between devices  48.9 us (5%)
  local copies, waits for them, and re-layouts  22.2 us (2%)
  matrix products  20.3 us (2%)
  other arithmetic  15.4 us (2%)
  between operations  15 us (2%)
    ppermute x10, waiting for transfers between devices, swapped(): return lax.ppermute(block, axis, route)  347 us
    psum x2, waiting for transfers between devices, layers(): raw, squares = lax.psum((raw, squares), 'tensor')  265 us
    psum x2, blocking collectives, layers(): raw, squares = lax.psum((raw, squares), 'tensor')  262 us
    ppermute x10, starting transfers between devices, swapped(): return lax.ppermute(block, axis, route)  38.4 us
  transfers between devices with their start and end apart: 16, of which 15 were waited for; matrix products, arithmetic and copies ran while one was open for 2% of the time, Pallas kernels for 0%

commit v1 on v0

v1 whole, which is shorter than its diff:
```python
import functools

import jax
import jax.numpy as jnp
from jax import lax
from jax.experimental import pallas as pl
from jax.experimental.pallas import tpu as pltpu
from jax.sharding import PartitionSpec as P

MESH = pl.DeviceIdType.MESH
TOK = 128
LAT = 512
LANES = 128
BLOCKS = LAT // LANES
eps = 1e-06
F32 = jnp.float32
BF16 = jnp.bfloat16

ROUNDS = {
    "a0": ("raw", "saved", "saved", "dm"),
    "b0": ("dm", "saved"),
    "b1": ("raw", "saved"),
    "a1": ("raw", "dm"),
    "b2": ("dm",),
    "b3": ("raw",),
}


def blocks_out(kinds):
    return BLOCKS * len(kinds) + (any(k != "dm" for k in kinds))


def blocks_back(kinds):
    return BLOCKS * len(kinds) + ("saved" in kinds)


def lane_pair(values, shape):
    lane = lax.broadcasted_iota(jnp.int32, shape, 1)
    block = jnp.zeros(shape, F32)
    for q, value in enumerate(values):
        high = value.astype(BF16).astype(F32)
        block = jnp.where(lane == 2 * q, high, jnp.where(lane == 2 * q + 1, value - high, block))
    return block.astype(BF16)


def from_pair(block, q):
    lane = lax.broadcasted_iota(jnp.int32, block.shape, 1)
    mine = (lane == 2 * q) | (lane == 2 * q + 1)
    return jnp.sum(jnp.where(mine, block, 0.0), axis=1, keepdims=True)


def dot(a, b, over=((1,), (0,))):
    return lax.dot_general(a, b, (over, ((), ())), preferred_element_type=F32)


NT = ((1,), (1,))
TN = ((0,), (0,))


def attend(latent):
    scores = dot(latent, latent, NT) * (4.0 / LAT)
    rows = lax.broadcasted_iota(jnp.int32, scores.shape, 0)
    cols = lax.broadcasted_iota(jnp.int32, scores.shape, 1)
    scores = jnp.where(rows >= cols, scores, -jnp.inf)
    top = jnp.max(scores, axis=1, keepdims=True)
    weights = jnp.exp(scores - top)
    probs = weights / jnp.sum(weights, axis=1, keepdims=True)
    probs_b = probs.astype(BF16)
    return probs, probs_b, dot(probs_b, latent).astype(BF16)


class Semaphores:
    def __init__(self, ref):
        self.ref, self.used = ref, 0

    def new(self):
        self.used += 1
        return self.ref.at[self.used - 1]


N_LOCAL, N_REMOTE = 48, 160


class Round:
    def __init__(self, kinds, refs, remote, mesh_at, width):
        self.kinds, self.width = kinds, width
        self.send, self.got, self.mine, self.other, self.full = refs
        self.pipe, self.half, self.j, self.group = mesh_at
        self.rows = TOK // self.group
        j, group = self.j, self.group
        self.own = pl.ds(pl.multiple_of(j * self.rows, self.rows), self.rows)
        self.scatter, self.gather, self.arrive = [], [], []
        for k in range(1, group):
            to = lax.rem(j + k, group)
            source = lax.rem(j - k + group, group)
            to_rows = pl.ds(pl.multiple_of(to * self.rows, self.rows), self.rows)
            from_rows = pl.ds(pl.multiple_of(source * self.rows, self.rows), self.rows)
            device = (self.pipe, self.half * group + to)
            self.scatter.append(remote(self.send.at[:, to_rows, :], self.got.at[k - 1], device))
            out = remote(self.full.at[:, self.own, :], self.full.at[:, self.own, :], device)
            self.gather.append(out)
            self.arrive.append(
                pltpu.make_async_remote_copy(
                    src_ref=self.full.at[:, from_rows, :],
                    dst_ref=self.full.at[:, from_rows, :],
                    send_sem=out.src_sem,
                    recv_sem=out.dst_sem,
                    device_id=device,
                    device_id_type=MESH,
                )
            )
        self.swap = remote(self.mine, self.other, (self.pipe, (1 - self.half) * group + j))

    def start(self, parts):
        norms = []
        for p, (value, norm) in enumerate(parts):
            for c in range(BLOCKS):
                self.send[p * BLOCKS + c] = value[:, c * LANES : (c + 1) * LANES].astype(BF16)
            if norm is not None:
                norms.append(norm)
        if norms:
            self.send[len(parts) * BLOCKS] = lane_pair(norms, (TOK, LANES))
        for copy in self.scatter:
            copy.start()

    def half_sum(self):
        for copy in self.scatter:
            copy.wait_recv()
        total = self.send[:, self.own, :].astype(F32)
        for k in range(self.group - 1):
            total = total + self.got[k].astype(F32)
        last = len(self.kinds) * BLOCKS
        self.mine[:last] = total[:last].astype(BF16)
        if blocks_out(self.kinds) > last:
            norms = [from_pair(total[last], q) for q in range(sum(k != "dm" for k in self.kinds))]
            self.mine[last] = lane_pair(norms, (self.rows, LANES))
        self.swap.start()

    def finish(self):
        self.swap.wait_recv()
        total = self.mine[...].astype(F32) + self.other[...].astype(F32)
        last = len(self.kinds) * BLOCKS
        raws, scales = 0, []
        for p, kind in enumerate(self.kinds):
            value = total[p * BLOCKS : (p + 1) * BLOCKS]
            if kind != "dm":
                scale = lax.rsqrt(from_pair(total[last], raws) / self.width + eps)
                raws += 1
                value = value * scale[None]
                if kind == "saved":
                    scales.append(scale)
            self.full[p * BLOCKS : (p + 1) * BLOCKS, self.own, :] = value.astype(BF16)
        if scales:
            self.full[last, self.own, :] = lane_pair(scales, (self.rows, LANES))
        for copy in self.gather:
            copy.start()

    def collect(self):
        for copy in self.arrive:
            copy.wait_recv()

    def part(self, p):
        return jnp.concatenate([self.full[p * BLOCKS + c] for c in range(BLOCKS)], axis=1)

    def scale(self, q):
        return from_pair(self.full[len(self.kinds) * BLOCKS].astype(F32), q)

    def drain(self):
        for copy in self.scatter + self.gather + [self.swap]:
            copy.wait_send()


def kernel(sections, shards, *refs):
    in_flight, entering, saved, down_in, back_in, outs, grads, g_down, g_back = refs[:9]
    down, back, xs, dys, kept, fs, gs, draws, mixes, sum_down, sum_back = refs[9:20]
    ssem, rsem, lsem = refs[-3:]
    buffers = refs[20:-3]
    group = shards // 2
    width = down.shape[0] * shards

    me = lax.axis_index("pipe")
    place = lax.axis_index("tensor")
    half, j = place // group, lax.rem(place, group)
    last = sections - 1
    sends, receives, locals_ = Semaphores(ssem), Semaphores(rsem), Semaphores(lsem)

    def remote(source, target, device):
        return pltpu.make_async_remote_copy(
            src_ref=source,
            dst_ref=target,
            send_sem=sends.new(),
            recv_sem=receives.new(),
            device_id=device,
            device_id_type=MESH,
        )

    def local(source, target):
        return pltpu.make_async_copy(source, target, locals_.new())

    not_first, not_last = me > 0, me < last
    nxt = (jnp.minimum(me + 1, last), place)
    prev = (jnp.maximum(me - 1, 0), place)
    across = (last - me, place)
    x_self, dy_self = me == sections // 2, me == sections // 2 - 1
    x_far = not_first & jnp.logical_not(x_self)
    dy_far = not_last & jnp.logical_not(dy_self)
    x_to = (jnp.where(x_far, sections - me, 0), place)
    dy_to = (jnp.where(dy_far, last - 1 - me, 0), place)

    load_down, load_back = local(down_in.at[0], down), local(back_in.at[0], back)
    load_kept = [local(saved.at[0, t], kept.at[0, t]) for t in range(2)]
    for copy in [load_down, load_back] + load_kept:
        copy.start()
    load_x = [local(entering.at[s, t], xs.at[s, t]) for s in range(2) for t in range(2)]
    load_dy = [local(entering.at[2 + s, t], dys.at[s, t]) for s in range(2) for t in range(2)]
    load_x_self = local(in_flight.at[1], xs.at[1, 0])
    load_dy_self = local(in_flight.at[3], dys.at[1, 0])

    def when_all(condition, copies, what):
        @pl.when(condition)
        def _():
            for copy in copies:
                getattr(copy, what)()

    when_all(me == 0, load_x, "start")
    when_all(me == last, load_dy, "start")
    when_all(x_self, [load_x_self], "start")
    when_all(dy_self, [load_dy_self], "start")

    barrier = pltpu.get_barrier_semaphore()

    def greet(device):
        pl.semaphore_signal(barrier, inc=1, device_id=device, device_id_type=MESH)

    for k in range(1, group):
        greet((me, half * group + lax.rem(j + k, group)))
    greet((me, (1 - half) * group + j))
    greet(across)
    count = group + 1
    for condition, device in ((not_last, nxt), (not_first, prev), (x_far, x_to), (dy_far, dy_to)):
        pl.when(condition)(functools.partial(greet, device))
        count = count + condition.astype(jnp.int32)
    pl.semaphore_wait(barrier, count)

    send_xa = remote(in_flight.at[0], xs.at[0, 0], nxt)
    send_dya = remote(in_flight.at[2], dys.at[0, 0], prev)
    send_dyb = remote(in_flight.at[3], dys.at[1, 0], dy_to)
    send_kept = [remote(saved.at[1, t], kept.at[1, t], across) for t in range(2)]
    send_xb = remote(in_flight.at[1], xs.at[1, 0], x_to)
    when_all(not_last, [send_xa], "start")
    when_all(not_first, [send_dya], "start")
    when_all(dy_far, [send_dyb], "start")
    send_kept[0].start()

    at = (me, half, j, group)
    rounds = {}
    for n, (name, kinds) in enumerate(ROUNDS.items()):
        rounds[name] = Round(kinds, buffers[5 * n : 5 * n + 5], remote, at, width)

    def raw_part(x):
        wide = x.astype(F32)
        return dot(x, down[...]), jnp.sum(wide * wide, axis=1, keepdims=True)

    def dm_part(dy):
        return dot(dy, back[...], NT), None

    def forward(x, mixed, slot):
        slot[...] = (x.astype(F32) + dot(mixed, back[...])).astype(BF16)

    def backward(s, t, saved_state, dmixed):
        latent, scale, probs, probs_b = saved_state
        dprobs = dot(dmixed, latent, NT)
        dscores = probs * (dprobs - jnp.sum(probs * dprobs, axis=1, keepdims=True))
        dsym = ((dscores + dscores.T) * (4.0 / LAT)).astype(BF16)
        dlatent = dot(dsym, latent) + dot(probs_b, dmixed, TN)
        draw = (dlatent * scale).astype(BF16)
        draws[s, t] = draw
        along = jnp.sum(dlatent * latent.astype(F32), axis=1, keepdims=True)
        result = dys[s, t].astype(F32) + dot(draw, down[...], NT)
        result = result - kept[s, t].astype(F32) * (scale * scale * along / width)
        gs[s, t] = result.astype(BF16)

    def recompute(s, t, latent, scale):
        probs, probs_b, mixed = attend(latent)
        mixes[s, t] = mixed
        return latent, scale, probs, probs_b

    def stream_grads(s):
        rows = (2 * TOK, LAT)
        cols = (2 * TOK, down.shape[0])
        return (
            dot(kept[s].reshape(cols), draws[s].reshape(rows), TN),
            dot(mixes[s].reshape(rows), dys[s].reshape(cols), TN),
        )

    shift_x = [remote(fs.at[s, 0], xs.at[s, 1], nxt) for s in range(2)]
    shift_dy = [remote(gs.at[s, 0], dys.at[s, 1], prev) for s in range(2)]
    out_f = [remote(fs.at[1, t], outs.at[1, t], across) for t in range(2)]
    out_g = [remote(gs.at[1, t], grads.at[1, t], across) for t in range(2)]
    keep_f = [local(fs.at[0, t], outs.at[0, t]) for t in range(2)]
    keep_g = [local(gs.at[0, t], grads.at[0, t]) for t in range(2)]

    load_down.wait()
    for copy in load_kept:
        copy.wait()
    parts = [raw_part(kept[0, t]) for t in range(2)]
    load_back.wait()
    when_all(me == 0, load_x, "wait")
    when_all(me == last, load_dy, "wait")
    when_all(x_self, [load_x_self], "wait")
    when_all(dy_self, [load_dy_self], "wait")
    when_all(not_first, [send_xa], "wait_recv")
    when_all(not_last, [send_dya], "wait_recv")
    rounds["a0"].start([raw_part(xs[0, 0])] + parts + [dm_part(dys[0, 0])])
    rounds["a0"].half_sum()

    when_all(dy_far, [send_dyb], "wait_recv")
    send_kept[0].wait_recv()
    when_all(x_far, [send_xb], "start")
    send_kept[1].start()
    rounds["b0"].start([dm_part(dys[1, 0]), raw_part(kept[1, 0])])
    rounds["a0"].finish()
    rounds["b0"].half_sum()

    rounds["a0"].collect()
    part = rounds["a0"].part
    forward(xs[0, 0], attend(part(0))[2], fs.at[0, 0])
    when_all(not_last, [shift_x[0]], "start")
    state = recompute(0, 0, part(1), rounds["a0"].scale(0))
    backward(0, 0, state, part(3))
    when_all(not_first, [shift_dy[0]], "start")
    keep_f[0].start()
    keep_g[0].start()
    state_a = recompute(0, 1, part(2), rounds["a0"].scale(1))

    when_all(not_first, [shift_x[0]], "wait_recv")
    when_all(not_last, [shift_dy[0]], "wait_recv")
    rounds["a1"].start([raw_part(xs[0, 1]), dm_part(dys[0, 1])])
    rounds["b0"].finish()
    rounds["a1"].half_sum()

    rounds["b0"].collect()
    state = recompute(1, 0, rounds["b0"].part(1), rounds["b0"].scale(0))
    backward(1, 0, state, rounds["b0"].part(0))
    when_all(not_first, [shift_dy[1]], "start")
    out_g[0].start()

    when_all(x_far, [send_xb], "wait_recv")
    send_kept[1].wait_recv()
    rounds["b1"].start([raw_part(xs[1, 0]), raw_part(kept[1, 1])])
    when_all(not_last, [shift_dy[1]], "wait_recv")
    rounds["b2"].start([dm_part(dys[1, 1])])
    rounds["b1"].half_sum()
    rounds["b2"].half_sum()

    rounds["a1"].finish()
    rounds["a1"].collect()
    forward(xs[0, 1], attend(rounds["a1"].part(0))[2], fs.at[0, 1])
    backward(0, 1, state_a, rounds["a1"].part(1))
    keep_f[1].start()
    keep_g[1].start()

    rounds["b1"].finish()
    rounds["b2"].finish()
    rounds["b1"].collect()
    forward(xs[1, 0], attend(rounds["b1"].part(0))[2], fs.at[1, 0])
    when_all(not_last, [shift_x[1]], "start")
    out_f[0].start()
    state_b = recompute(1, 1, rounds["b1"].part(1), rounds["b1"].scale(0))
    rounds["b2"].collect()
    backward(1, 1, state_b, rounds["b2"].part(0))
    out_g[1].start()
    when_all(not_first, [shift_x[1]], "wait_recv")
    rounds["b3"].start([raw_part(xs[1, 1])])
    rounds["b3"].half_sum()

    own, far = stream_grads(0), stream_grads(1)
    for target, first, second in zip((sum_down, sum_back), own, far, strict=True):
        target[...] = (first.astype(BF16).astype(F32) + second.astype(BF16).astype(F32)).astype(BF16)
    keep_down, keep_back = local(sum_down, g_down.at[0]), local(sum_back, g_back.at[0])
    keep_down.start()
    keep_back.start()

    rounds["b3"].finish()
    rounds["b3"].collect()
    forward(xs[1, 1], attend(rounds["b3"].part(0))[2], fs.at[1, 1])
    out_f[1].start()

    for copy in keep_f + keep_g + [keep_down, keep_back]:
        copy.wait()
    for copy in out_f + out_g:
        copy.wait()
    for copy in send_kept:
        copy.wait_send()
    for item in rounds.values():
        item.drain()
    when_all(not_last, [send_xa] + shift_x, "wait_send")
    when_all(not_first, [send_dya] + shift_dy, "wait_send")
    when_all(x_far, [send_xb], "wait_send")
    when_all(dy_far, [send_dyb], "wait_send")


def solution(mesh):
    sections, shards = mesh.shape["pipe"], mesh.shape["tensor"]
    group = shards // 2
    rows = TOK // group

    def step(in_flight, entering, saved_inputs, latent_down, latent_back):
        local = latent_down.shape[1]
        act = pltpu.VMEM((2, 2, TOK, local), BF16)
        state = pltpu.VMEM((2, 2, TOK, LAT), BF16)
        buffers = []
        for kinds in ROUNDS.values():
            sent, returned = blocks_out(kinds), blocks_back(kinds)
            buffers += [
                pltpu.VMEM((sent, TOK, LANES), BF16),
                pltpu.VMEM((group - 1, sent, rows, LANES), BF16),
                pltpu.VMEM((sent, rows, LANES), BF16),
                pltpu.VMEM((sent, rows, LANES), BF16),
                pltpu.VMEM((returned, TOK, LANES), BF16),
            ]
        anywhere = pl.BlockSpec(memory_space=pl.ANY)
        return pl.pallas_call(
            functools.partial(kernel, sections, shards),
            out_shape=(
                jax.ShapeDtypeStruct((2, 2, TOK, local), BF16),
                jax.ShapeDtypeStruct((2, 2, TOK, local), BF16),
                jax.ShapeDtypeStruct((1, local, LAT), BF16),
                jax.ShapeDtypeStruct((1, LAT, local), BF16),
            ),
            in_specs=[anywhere] * 5,
            out_specs=[anywhere] * 4,
            scratch_shapes=[
                pltpu.VMEM((local, LAT), BF16),
                pltpu.VMEM((LAT, local), BF16),
                *[act] * 5,
                *[state] * 2,
                pltpu.VMEM((local, LAT), BF16),
                pltpu.VMEM((LAT, local), BF16),
                *buffers,
                pltpu.SemaphoreType.DMA((N_REMOTE,)),
                pltpu.SemaphoreType.DMA((N_REMOTE,)),
                pltpu.SemaphoreType.DMA((N_LOCAL,)),
            ],
            compiler_params=pltpu.CompilerParams(
                collective_id=0, has_side_effects=True, vmem_limit_bytes=40 * 2**20
            ),
        )(in_flight, entering, saved_inputs, latent_down, latent_back)

    return jax.shard_map(
        step,
        mesh=mesh,
        in_specs=(
            P(None, "pipe", "tensor"),
            P(None, None, None, "tensor"),
            P(None, None, "pipe", "tensor"),
            P("pipe", "tensor", None),
            P("pipe", None, "tensor"),
        ),
        out_specs=(
            P(None, None, "pipe", "tensor"),
            P(None, None, "pipe", "tensor"),
            P("pipe", "tensor", None),
            P("pipe", None, "tensor"),
        ),
        check_vma=False,
    )
```

time: 1000 us -> 185 us (0.18)
  the two profiles are of different devices: /device:TPU:25 before, /device:TPU:102 now
where the time goes in v1:
time: 185 us
  Pallas kernels  173 us (94%)
  local copies, waits for them, and re-layouts  11.2 us (6%)
    pallas_call x1, Pallas kernels, step(): pl.pallas_call(functools.partial(kernel, sections, shards), out_shape=(ja...  173 us
    unnamed x23, local copies, waits for them, and re-layouts  7.15 us
    pallas_call x3, local copies, waits for them, and re-layouts, step(): pl.pallas_call(functools.partial(kernel, sections, shards), out_shape=(ja...  4 us

profile of v1, /device:TPU:102, one launch (start us, length us, event | category | flops | bytes accessed | tf_op | source)
XLA Modules:
  0.0 185.0 jit_solution(9213455091530340716)
XLA Ops:
  0.6 0.0 copy-start.7
  0.6 0.0 copy-start.8
  0.7 1.3 copy.9.refs_0_
  2.0 0.0 copy-done.7
  2.0 0.0 copy-start.6
  2.0 0.2 copy.11.refs_2_
  2.2 0.0 copy-done.8
  2.2 0.2 copy.12.refs_4_
  2.4 0.7 copy-done.6
  3.1 0.5 copy.10.refs_1_
  3.7 0.0 copy-start.5
  3.7 1.0 copy-done.5
  4.7 173.1 %shard_map.84 = (bf16[2,2,128,448]{3,2,1,0:T(8,128)(2,1)S(1)}, bf16[2,2,128,448]{3,2,1,0:T(8,128)(2,1)S(1)}, bf16[1,448,512]{2,1,0:T(8,128)(2,1)S(1)}, bf16[1,512,448]{2,1,0:T(8,128)(2,1)S(1)}) custom-call(bf16[4,128,448]{2,1,0:T(8,128)(2,1)S(1)} %copy.9.refs_0_, bf16[4,2,128,448]{3,2,1,0:T(8,128)(2,1)S(1)} %copy.10.refs_1_, ...), custom_call_target="tpu_custom_call" | custom-call | tf_op jit(solution)/shard_map/pallas_call | solution.py:423
  177.8 0.0 copy-start
  177.9 0.8 copy-done
  178.6 0.0 copy-start.2
  178.6 0.8 copy-done.2
  179.4 0.0 copy-start.3
  179.4 0.8 copy-done.3
  180.2 0.0 copy-start.1
  180.2 2.1 %copy.13 = bf16[2,2,128,448]{2,3,1,0:T(8,128)(2,1)} copy(bf16[2,2,128,448]{3,2,1,0:T(8,128)(2,1)} %copy-done.2) | data formatting | bytes 917504 | tf_op jit(solution)/shard_map/pallas_call | solution.py:423
  182.3 0.0 copy-done.1
  182.3 1.0 copy.14
  183.2 0.0 copy-start.4
  183.2 1.0 copy.15
  184.2 0.1 copy-done.4
  184.3 0.8 copy.17
Async XLA Ops:
  0.6 1.3 copy-start.7
  0.6 1.6 copy-start.8
  2.0 1.2 copy-start.6
  3.7 1.0 copy-start.5
  177.8 0.8 copy-start
  178.6 0.8 copy-start.2
  179.4 0.8 copy-start.3
  180.2 2.1 %copy-start.1 = (bf16[2,2,128,448]{3,2,1,0:T(8,128)(2,1)S(1)}, bf16[2,2,128,448]{3,2,1,0:T(8,128)(2,1)}, u32[]{:S(2)}) copy-start(bf16[2,2,128,448]{3,2,1,0:T(8,128)(2,1)} %copy-done) | copy-start | bytes 1376260
  183.2 1.0 copy-start.4

commit v2 on v1

v2 whole, which is shorter than its diff:
```python
import functools

import jax
import jax.numpy as jnp
from jax import lax
from jax.experimental import pallas as pl
from jax.experimental.pallas import tpu as pltpu
from jax.sharding import PartitionSpec as P


MESH = pl.DeviceIdType.MESH
TOK = 128
LAT = 512
NORM_ROWS = 16
eps = 1e-06
F32 = jnp.float32
BF16 = jnp.bfloat16
NN = ((1,), (0,))
NT = ((1,), (1,))
TN = ((0,), (0,))

ROUNDS = {
    "a0": ("raw", "raw", "dm"),
    "b0": ("raw", "raw", "dm"),
    "a1": ("raw", "raw", "dm"),
    "b1": ("raw", "raw", "dm"),
}
N_LOCAL, N_REMOTE = 48, 160

(
    ENTERED, A0_HERE, A0_SCATTERED, A0_SWAPPED, A0_GATHERED, A0_DONE, B0_SCATTERED, B0_SWAPPED,
    B0_GATHERED, B0_COLLECTED, B0_DONE, A1_SCATTERED, B1_HERE, B1_SCATTERED, B1_SWAPPED,
    B1_GATHERED, B1_COLLECTED, F1_DONE, B1_DONE,
) = range(19)
SCHEDULE = {
    "in": (ENTERED, A0_SWAPPED, A0_SWAPPED, A0_SWAPPED),
    "kept": (ENTERED, B0_GATHERED, B0_GATHERED, B0_GATHERED),
    "f0": (A1_SCATTERED, B1_SCATTERED, B1_SCATTERED, B1_SCATTERED),
    "g0": (B1_COLLECTED, B1_COLLECTED, B1_COLLECTED, B1_COLLECTED),
    "f1": (F1_DONE, F1_DONE, F1_DONE, F1_DONE),
    "g1": (B1_DONE, B1_DONE, B1_DONE, B1_DONE),
}


def due(item, off, n):
    classes = [c for c, start in enumerate(SCHEDULE[item]) if start == n]
    if not classes:
        return None
    now = off == classes[0]
    for c in classes[1:]:
        now = now | (off == c)
    return now


def chunk_rows(kinds, rows):
    return rows * len(kinds) + NORM_ROWS * ("raw" in kinds)


def dot(a, b, over=NN):
    return lax.dot_general(a, b, (over, ((), ())), preferred_element_type=F32)


def norm_block(norms):
    row = lax.broadcasted_iota(jnp.int32, (NORM_ROWS, TOK), 0)
    block = jnp.zeros((NORM_ROWS, TOK), F32)
    for q, value in enumerate(norms):
        high = value.astype(BF16).astype(F32)
        block = jnp.where(row == 2 * q, high, jnp.where(row == 2 * q + 1, value - high, block))
    return block.astype(BF16)


def norms_of(block, count):
    return [block[2 * q : 2 * q + 1] + block[2 * q + 1 : 2 * q + 2] for q in range(count)]


def attend(latent):
    scores = dot(latent, latent, TN) * (4.0 / LAT)
    key = lax.broadcasted_iota(jnp.int32, scores.shape, 0)
    query = lax.broadcasted_iota(jnp.int32, scores.shape, 1)
    scores = jnp.where(query >= key, scores, -jnp.inf)
    weights = jnp.exp(scores - jnp.max(scores, axis=0, keepdims=True))
    probs = weights / jnp.sum(weights, axis=0, keepdims=True)
    probs_b = probs.astype(BF16)
    return probs, probs_b, dot(latent, probs_b).astype(BF16)


class Semaphores:
    def __init__(self, ref):
        self.ref, self.used = ref, 0

    def new(self):
        self.used += 1
        return self.ref.at[self.used - 1]


class Round:
    def __init__(self, kinds, refs, remote, mesh_at, width):
        self.kinds, self.width = kinds, width
        self.send, self.got, self.mine, self.other, self.full = refs
        self.pipe, self.half, self.j, self.group = mesh_at
        self.rows = LAT // self.group
        self.raws = sum(k == "raw" for k in kinds)
        j, group = self.j, self.group
        own = pl.ds(pl.multiple_of(j * self.rows, self.rows), self.rows)
        self.own = own
        self.scatter, self.gather, self.arrive = [], [], []
        for k in range(1, group):
            to = lax.rem(j + k, group)
            source = lax.rem(j - k + group, group)
            theirs = pl.ds(pl.multiple_of(source * self.rows, self.rows), self.rows)
            device = (self.pipe, self.half * group + to)
            self.scatter.append(remote(self.send.at[to], self.got.at[k - 1], device))
            out = remote(self.full.at[:, own, :], self.full.at[:, own, :], device)
            self.gather.append(out)
            self.arrive.append(
                pltpu.make_async_remote_copy(
                    src_ref=self.full.at[:, theirs, :],
                    dst_ref=self.full.at[:, theirs, :],
                    send_sem=out.src_sem,
                    recv_sem=out.dst_sem,
                    device_id=device,
                    device_id_type=MESH,
                )
            )
        self.swap = remote(self.mine, self.other, (self.pipe, (1 - self.half) * group + j))

    def start(self, parts):
        rows = self.rows
        norms = [norm for _, norm in parts if norm is not None]
        for p, (value, _) in enumerate(parts):
            value = value.astype(BF16)
            for g in range(self.group):
                self.send[g, p * rows : (p + 1) * rows] = value[g * rows : (g + 1) * rows]
        if norms:
            block = norm_block(norms)
            for g in range(self.group):
                self.send[g, len(parts) * rows :] = block
        for copy in self.scatter:
            copy.start()

    def half_sum(self):
        for copy in self.scatter:
            copy.wait_recv()
        total = self.send[self.j].astype(F32)
        for k in range(self.group - 1):
            total = total + self.got[k].astype(F32)
        last = len(self.kinds) * self.rows
        self.mine[:last] = total[:last].astype(BF16)
        if self.raws:
            self.mine[last:] = norm_block(norms_of(total[last:], self.raws))
        self.swap.start()

    def finish(self):
        self.swap.wait_recv()
        total = self.mine[...].astype(F32) + self.other[...].astype(F32)
        rows = self.rows
        scales, raw = self.scales_of(total), 0
        for p, kind in enumerate(self.kinds):
            value = total[p * rows : (p + 1) * rows]
            if kind == "raw":
                value = value * scales[raw]
                raw += 1
            self.full[p, self.own, :] = value.astype(BF16)
        for copy in self.gather:
            copy.start()

    def scales_of(self, total):
        norms = norms_of(total[len(self.kinds) * self.rows :], self.raws) if self.raws else []
        return [lax.rsqrt(norm / self.width + eps) for norm in norms]

    @property
    def scales(self):
        return self.scales_of(self.mine[...].astype(F32) + self.other[...].astype(F32))

    def collect(self):
        for copy in self.arrive:
            copy.wait_recv()

    def part(self, p):
        return self.full[p]

    def drain(self):
        for copy in self.scatter + self.gather + [self.swap]:
            copy.wait_send()


def kernel(sections, shards, *refs):
    in_flight, entering, saved, down_in, back_in, outs, grads, g_down, g_back = refs[:9]
    down, back, down_t, back_t, xs, dys, kept, fs, gs, draws, mixes, sum_down, sum_back = refs[9:22]
    ssem, rsem, lsem = refs[-3:]
    buffers = refs[22:-3]
    group = shards // 2
    width = down.shape[0] * shards

    me = lax.axis_index("pipe")
    place = lax.axis_index("tensor")
    half, j = place // group, lax.rem(place, group)
    last = sections - 1
    sends, receives, locals_ = Semaphores(ssem), Semaphores(rsem), Semaphores(lsem)

    def remote(source, target, device):
        return pltpu.make_async_remote_copy(
            src_ref=source,
            dst_ref=target,
            send_sem=sends.new(),
            recv_sem=receives.new(),
            device_id=device,
            device_id_type=MESH,
        )

    def local(source, target):
        return pltpu.make_async_copy(source, target, locals_.new())

    not_first, not_last = me > 0, me < last
    nxt = (jnp.minimum(me + 1, last), place)
    prev = (jnp.maximum(me - 1, 0), place)
    across = (last - me, place)
    x_self, dy_self = me == sections // 2, me == sections // 2 - 1
    x_far = not_first & jnp.logical_not(x_self)
    dy_far = not_last & jnp.logical_not(dy_self)
    x_to = (jnp.where(x_far, sections - me, 0), place)
    dy_to = (jnp.where(dy_far, last - 1 - me, 0), place)

    load_down, load_back = local(down_in.at[0], down), local(back_in.at[0], back)
    load_kept = [local(saved.at[0, t], kept.at[0, t]) for t in range(2)]
    for copy in [load_down, load_back] + load_kept:
        copy.start()
    load_x = [local(entering.at[s, t], xs.at[s, t]) for s in range(2) for t in range(2)]
    load_dy = [local(entering.at[2 + s, t], dys.at[s, t]) for s in range(2) for t in range(2)]
    load_x_self = local(in_flight.at[1], xs.at[1, 0])
    load_dy_self = local(in_flight.at[3], dys.at[1, 0])

    def when_all(condition, copies, what):
        @pl.when(condition)
        def _():
            for copy in copies:
                getattr(copy, what)()

    when_all(me == 0, load_x, "start")
    when_all(me == last, load_dy, "start")
    when_all(x_self, [load_x_self], "start")
    when_all(dy_self, [load_dy_self], "start")

    def raw_part(x):
        wide = x.astype(F32)
        return dot(down_t[...], x), jnp.sum(wide * wide, axis=0, keepdims=True)

    barrier = pltpu.get_barrier_semaphore()

    def greet(device):
        pl.semaphore_signal(barrier, inc=1, device_id=device, device_id_type=MESH)

    for k in range(1, group):
        greet((me, half * group + lax.rem(j + k, group)))
    greet((me, (1 - half) * group + j))
    greet(across)
    count = group + 1
    for condition, device in ((not_last, nxt), (not_first, prev), (x_far, x_to), (dy_far, dy_to)):
        pl.when(condition)(functools.partial(greet, device))
        count = count + condition.astype(jnp.int32)
    load_down.wait()
    load_back.wait()
    down_t[...] = down[...].T
    back_t[...] = back[...].T
    for copy in load_kept:
        copy.wait()
    kept_parts = [raw_part(kept[0, t]) for t in range(2)]
    when_all(me == 0, load_x, "wait")
    when_all(me == last, load_dy, "wait")
    when_all(x_self, [load_x_self], "wait")
    when_all(dy_self, [load_dy_self], "wait")
    pl.semaphore_wait(barrier, count)

    send_xa = remote(in_flight.at[0], xs.at[0, 0], nxt)
    send_dya = remote(in_flight.at[2], dys.at[0, 0], prev)
    send_dyb = remote(in_flight.at[3], dys.at[1, 0], dy_to)
    send_kept = [remote(saved.at[1, t], kept.at[1, t], across) for t in range(2)]
    send_xb = remote(in_flight.at[1], xs.at[1, 0], x_to)
    when_all(not_last, [send_xa], "start")
    when_all(not_first, [send_dya], "start")
    at = (me, half, j, group)
    rounds = {}
    for n, (name, kinds) in enumerate(ROUNDS.items()):
        rounds[name] = Round(kinds, buffers[5 * n : 5 * n + 5], remote, at, width)

    def dm_part(dy):
        return dot(back_t[...], dy), None

    def forward(x, mixed, slot):
        slot[...] = (x.astype(F32) + dot(back[...], mixed)).astype(BF16)

    def backward(s, t, state, dmixed):
        latent, scale, probs, probs_b = state
        dprobs = dot(latent, dmixed, TN)
        dscores = probs * (dprobs - jnp.sum(probs * dprobs, axis=0, keepdims=True))
        dsym = ((dscores + dscores.T) * (4.0 / LAT)).astype(BF16)
        dlatent = dot(latent, dsym) + dot(dmixed, probs_b, NT)
        draw = (dlatent * scale).astype(BF16)
        draws[s, t] = draw
        along = jnp.sum(dlatent * latent.astype(F32), axis=0, keepdims=True)
        result = dys[s, t].astype(F32) + dot(down[...], draw)
        result = result - kept[s, t].astype(F32) * (scale * scale * along / width)
        gs[s, t] = result.astype(BF16)

    def recompute(s, t, latent, scale):
        probs, probs_b, mixed = attend(latent)
        mixes[s, t] = mixed
        return latent, scale, probs, probs_b

    def add_grads(s):
        for target, left, right in ((sum_down, kept, draws), (sum_back, dys, mixes)):
            total = dot(left[s, 0], right[s, 0], NT) + dot(left[s, 1], right[s, 1], NT)
            total = total.astype(BF16)
            if s == 1:
                total = (target[...].astype(F32) + total.astype(F32)).astype(BF16)
            target[...] = total

    shift_x = [remote(fs.at[s, 0], xs.at[s, 1], nxt) for s in range(2)]
    shift_dy = [remote(gs.at[s, 0], dys.at[s, 1], prev) for s in range(2)]
    out_f = [remote(fs.at[1, t], outs.at[1, t], across) for t in range(2)]
    out_g = [remote(gs.at[1, t], grads.at[1, t], across) for t in range(2)]
    keep_f = [local(fs.at[0, t], outs.at[0, t]) for t in range(2)]
    keep_g = [local(gs.at[0, t], grads.at[0, t]) for t in range(2)]

    off = jnp.where(me < sections // 2, sections // 2 - 1 - me, me - sections // 2) // max(sections // 8, 1)

    everyone = [(None, copy) for copy in send_kept]
    bulk = {
        "in": [(x_far, send_xb), (dy_far, send_dyb), everyone[0]],
        "kept": [everyone[1]],
        "f0": [(None, out_f[0])],
        "g0": [(None, out_g[0])],
        "f1": [(None, out_f[1])],
        "g1": [(None, out_g[1])],
    }

    def point(n):
        for item, copies in bulk.items():
            now = due(item, off, n)
            if now is None:
                continue

            @pl.when(now)
            def _():
                for condition, copy in copies:
                    if condition is None:
                        copy.start()
                    else:
                        when_all(condition, [copy], "start")

    a0, b0, a1, b1 = (rounds[name] for name in ROUNDS)

    def take_b0():
        when_all(x_far, [send_xb], "wait_recv")
        when_all(dy_far, [send_dyb], "wait_recv")
        send_kept[0].wait_recv()
        b0.start([raw_part(xs[1, 0]), raw_part(kept[1, 0]), dm_part(dys[1, 0])])
        point(B0_SCATTERED)

    point(ENTERED)
    when_all(not_first, [send_xa], "wait_recv")
    when_all(not_last, [send_dya], "wait_recv")
    point(A0_HERE)
    a0.start([raw_part(xs[0, 0]), kept_parts[0], dm_part(dys[0, 0])])
    point(A0_SCATTERED)
    a0.half_sum()
    point(A0_SWAPPED)
    take_b0()
    a0.finish()
    point(A0_GATHERED)
    b0.half_sum()
    point(B0_SWAPPED)
    a0.collect()
    forward(xs[0, 0], attend(a0.part(0))[2], fs.at[0, 0])
    when_all(not_last, [shift_x[0]], "start")
    backward(0, 0, recompute(0, 0, a0.part(1), a0.scales[1]), a0.part(2))
    when_all(not_first, [shift_dy[0]], "start")
    keep_f[0].start()
    keep_g[0].start()
    point(A0_DONE)
    b0.finish()
    point(B0_GATHERED)
    b0.collect()
    point(B0_COLLECTED)
    forward(xs[1, 0], attend(b0.part(0))[2], fs.at[1, 0])
    when_all(not_last, [shift_x[1]], "start")
    backward(1, 0, recompute(1, 0, b0.part(1), b0.scales[1]), b0.part(2))
    when_all(not_first, [shift_dy[1]], "start")
    point(B0_DONE)

    when_all(not_first, [shift_x[0]], "wait_recv")
    when_all(not_last, [shift_dy[0]], "wait_recv")
    a1.start([raw_part(xs[0, 1]), kept_parts[1], dm_part(dys[0, 1])])
    point(A1_SCATTERED)
    when_all(not_first, [shift_x[1]], "wait_recv")
    when_all(not_last, [shift_dy[1]], "wait_recv")
    point(B1_HERE)
    send_kept[1].wait_recv()
    b1.start([raw_part(xs[1, 1]), raw_part(kept[1, 1]), dm_part(dys[1, 1])])
    point(B1_SCATTERED)
    a1.half_sum()
    b1.half_sum()
    point(B1_SWAPPED)
    a1.finish()
    b1.finish()
    point(B1_GATHERED)
    a1.collect()
    forward(xs[0, 1], attend(a1.part(0))[2], fs.at[0, 1])
    keep_f[1].start()
    backward(0, 1, recompute(0, 1, a1.part(1), a1.scales[1]), a1.part(2))
    keep_g[1].start()
    add_grads(0)
    b1.collect()
    point(B1_COLLECTED)
    forward(xs[1, 1], attend(b1.part(0))[2], fs.at[1, 1])
    point(F1_DONE)
    backward(1, 1, recompute(1, 1, b1.part(1), b1.scales[1]), b1.part(2))
    point(B1_DONE)
    add_grads(1)
    keep_down, keep_back = local(sum_down, g_down.at[0]), local(sum_back, g_back.at[0])
    keep_down.start()
    keep_back.start()

    for copy in keep_f + keep_g + [keep_down, keep_back]:
        copy.wait()
    for copy in send_kept:
        copy.wait_send()
    for item in rounds.values():
        item.drain()
    when_all(not_last, [send_xa], "wait_send")
    when_all(not_first, [send_dya], "wait_send")
    when_all(not_last, shift_x, "wait_send")
    when_all(not_first, shift_dy, "wait_send")
    when_all(x_far, [send_xb], "wait_send")
    when_all(dy_far, [send_dyb], "wait_send")
    for copy in out_f + out_g:
        copy.wait()


def hand_out(*refs):
    sources, targets, stages, sems = refs[:4], refs[4:8], refs[8:12], refs[12]
    loads, stores = [], []
    for source, target, stage in zip(sources, targets, stages, strict=True):
        for part in range(source.shape[0]):
            n = len(loads)
            loads.append(pltpu.make_async_copy(source.at[part], stage.at[part], sems.at[2 * n]))
            stores.append(pltpu.make_async_copy(stage.at[part], target.at[part], sems.at[2 * n + 1]))
    for load in loads:
        load.start()
    for load, store in zip(loads, stores, strict=True):
        load.wait()
        store.start()
    for store in stores:
        store.wait()


def solution(mesh):
    sections, shards = mesh.shape["pipe"], mesh.shape["tensor"]
    group = shards // 2
    rows = LAT // group

    def step(in_flight, entering, saved_inputs, latent_down, latent_back):
        local = latent_down.shape[1]
        act = pltpu.VMEM((2, 2, local, TOK), BF16)
        state = pltpu.VMEM((2, 2, LAT, TOK), BF16)
        buffers = []
        for kinds in ROUNDS.values():
            chunk = chunk_rows(kinds, rows)
            buffers += [
                pltpu.VMEM((group, chunk, TOK), BF16),
                pltpu.VMEM((group - 1, chunk, TOK), BF16),
                pltpu.VMEM((chunk, TOK), BF16),
                pltpu.VMEM((chunk, TOK), BF16),
                pltpu.VMEM((len(kinds), LAT, TOK), BF16),
            ]
        anywhere = pl.BlockSpec(memory_space=pl.ANY)
        results = (
            jax.ShapeDtypeStruct((2, 2, local, TOK), BF16),
            jax.ShapeDtypeStruct((2, 2, local, TOK), BF16),
            jax.ShapeDtypeStruct((1, local, LAT), BF16),
            jax.ShapeDtypeStruct((1, local, LAT), BF16),
        )
        made = pl.pallas_call(
            functools.partial(kernel, sections, shards),
            out_shape=results,
            in_specs=[anywhere] * 5,
            out_specs=[anywhere] * 4,
            scratch_shapes=[
                *[pltpu.VMEM((local, LAT), BF16)] * 2,
                *[pltpu.VMEM((LAT, local), BF16)] * 2,
                *[act] * 5,
                *[state] * 2,
                *[pltpu.VMEM((local, LAT), BF16)] * 2,
                *buffers,
                pltpu.SemaphoreType.DMA((N_REMOTE,)),
                pltpu.SemaphoreType.DMA((N_REMOTE,)),
                pltpu.SemaphoreType.DMA((N_LOCAL,)),
            ],
            compiler_params=pltpu.CompilerParams(
                collective_id=0, has_side_effects=True, vmem_limit_bytes=60 * 2**20
            ),
        )(
            jnp.swapaxes(in_flight, 1, 2),
            jnp.swapaxes(entering, 2, 3),
            jnp.swapaxes(saved_inputs, 2, 3),
            latent_down,
            jnp.swapaxes(latent_back, 1, 2),
        )
        outs, grads, grad_down, grad_back = pl.pallas_call(
            hand_out,
            out_shape=results,
            in_specs=[anywhere] * 4,
            out_specs=[anywhere] * 4,
            scratch_shapes=[
                *[pltpu.VMEM(result.shape, BF16) for result in results],
                pltpu.SemaphoreType.DMA((12,)),
            ],
            compiler_params=pltpu.CompilerParams(vmem_limit_bytes=60 * 2**20),
        )(*made)
        return (
            jnp.swapaxes(outs, 2, 3),
            jnp.swapaxes(grads, 2, 3),
            grad_down,
            jnp.swapaxes(grad_back, 1, 2),
        )

    return jax.shard_map(
        step,
        mesh=mesh,
        in_specs=(
            P(None, "pipe", "tensor"),
            P(None, None, None, "tensor"),
            P(None, None, "pipe", "tensor"),
            P("pipe", "tensor", None),
            P("pipe", None, "tensor"),
        ),
        out_specs=(
            P(None, None, "pipe", "tensor"),
            P(None, None, "pipe", "tensor"),
            P("pipe", "tensor", None),
            P("pipe", None, "tensor"),
        ),
        check_vma=False,
    )
```

time: 185 us -> 143 us (0.77)
  the two profiles are of different devices: /device:TPU:102 before, /device:TPU:129 now
where the time goes in v2:
time: 143 us; the launch traced here: 142 us
  Pallas kernels  142 us (99%)
    pallas_call x1, Pallas kernels, step(): pl.pallas_call(functools.partial(kernel, sections, shards), out_shape=res...  139 us

profile of v2, /device:TPU:129, one launch (start us, length us, event | category | flops | bytes accessed | tf_op | source)
XLA Modules:
  0.0 142.5 jit_solution(2816555056631467922)
XLA Ops:
  0.6 139.4 %shard_map.84 = (bf16[2,2,448,128]{3,2,1,0:T(8,128)(2,1)}, bf16[2,2,448,128]{3,2,1,0:T(8,128)(2,1)}, bf16[1,448,512]{2,1,0:T(8,128)(2,1)}, bf16[1,448,512]{2,1,0:T(8,128)(2,1)}) custom-call(bf16[4,448,128]{2,1,0:T(8,128)(2,1)} %bitcast.8, bf16[4,2,448,128]{3,2,1,0:T(8,128)(2,1)} %bitcast.7, bf16[2,2,448,128]{3,2,1,0:T(8,128)(2,1)} %bitcast.9, ...), custom_call_target="tpu_custom_call" | custom-call | tf_op jit(solution)/shard_map/pallas_call | solution.py:483
  140.0 2.5 %shard_map.85 = (bf16[2,2,448,128]{3,2,1,0:T(8,128)(2,1)}, bf16[2,2,448,128]{3,2,1,0:T(8,128)(2,1)}, bf16[1,448,512]{2,1,0:T(8,128)(2,1)}, bf16[1,448,512]{2,1,0:T(8,128)(2,1)}) custom-call(bf16[2,2,448,128]{3,2,1,0:T(8,128)(2,1)} %get-tuple-element.12.refs_0_, bf16[2,2,448,128]{3,2,1,0:T(8,128)(2,1)} %get-tuple-element.13.refs_1_, ...), custom_call_target="tpu_custom_call" | custom-call | tf_op jit(solution)/shard_map/pallas_call | solution.py:509

commit v3 on v2

--- a/solution.py
+++ b/solution.py
@@ -33,10 +33,10 @@
     B1_GATHERED, B1_COLLECTED, F1_DONE, B1_DONE,
 ) = range(19)
 SCHEDULE = {
-    "in": (ENTERED, A0_SWAPPED, A0_SWAPPED, A0_SWAPPED),
+    "in": (ENTERED, A0_SWAPPED, A0_SWAPPED, A0_HERE),
     "kept": (ENTERED, B0_GATHERED, B0_GATHERED, B0_GATHERED),
-    "f0": (A1_SCATTERED, B1_SCATTERED, B1_SCATTERED, B1_SCATTERED),
-    "g0": (B1_COLLECTED, B1_COLLECTED, B1_COLLECTED, B1_COLLECTED),
+    "f0": (B1_COLLECTED, A1_SCATTERED, B0_DONE, B0_DONE),
+    "g0": (B1_GATHERED, B1_GATHERED, B1_SWAPPED, B0_DONE),
     "f1": (F1_DONE, F1_DONE, F1_DONE, F1_DONE),
     "g1": (B1_DONE, B1_DONE, B1_DONE, B1_DONE),
 }
@@ -104,24 +104,39 @@
         own = pl.ds(pl.multiple_of(j * self.rows, self.rows), self.rows)
         self.own = own
         self.scatter, self.gather, self.arrive = [], [], []
+        self.relay, self.arrive_late = [], []
+
+        def rows_of(device):
+            return pl.ds(pl.multiple_of(device * self.rows, self.rows), self.rows)
+
+        def arrival(out, part):
+            return pltpu.make_async_remote_copy(
+                src_ref=part,
+                dst_ref=part,
+                send_sem=out.src_sem,
+                recv_sem=out.dst_sem,
+                device_id=sibling,
+                device_id_type=MESH,
+            )
+
         for k in range(1, group):
             to = lax.rem(j + k, group)
-            source = lax.rem(j - k + group, group)
-            theirs = pl.ds(pl.multiple_of(source * self.rows, self.rows), self.rows)
             device = (self.pipe, self.half * group + to)
             self.scatter.append(remote(self.send.at[to], self.got.at[k - 1], device))
-            out = remote(self.full.at[:, own, :], self.full.at[:, own, :], device)
+        other = j + 1 - 2 * lax.rem(j, 2)
+        sibling = (self.pipe, self.half * group + other)
+        mine = self.full.at[:, own, :]
+        self.gather.append(remote(mine, mine, sibling))
+        self.arrive_late.append(arrival(self.gather[0], self.full.at[:, rows_of(other), :]))
+        for k in range(2, group, 2):
+            to, source = lax.rem(j + k, group), lax.rem(j - k + group, group)
+            out = remote(mine, mine, (self.pipe, self.half * group + to))
             self.gather.append(out)
-            self.arrive.append(
-                pltpu.make_async_remote_copy(
-                    src_ref=self.full.at[:, theirs, :],
-                    dst_ref=self.full.at[:, theirs, :],
-                    send_sem=out.src_sem,
-                    recv_sem=out.dst_sem,
-                    device_id=device,
-                    device_id_type=MESH,
-                )
-            )
+            theirs = self.full.at[:, rows_of(source), :]
+            self.arrive.append(arrival(out, theirs))
+            self.relay.append(remote(theirs, theirs, sibling))
+            far = self.full.at[:, rows_of(lax.rem(other - k + group, group)), :]
+            self.arrive_late.append(arrival(self.relay[-1], far))
         self.swap = remote(self.mine, self.other, (self.pipe, (1 - self.half) * group + j))
 
     def start(self, parts):
@@ -173,14 +188,17 @@
         return self.scales_of(self.mine[...].astype(F32) + self.other[...].astype(F32))
 
     def collect(self):
-        for copy in self.arrive:
+        for copy, onward in zip(self.arrive, self.relay, strict=True):
+            copy.wait_recv()
+            onward.start()
+        for copy in self.arrive_late:
             copy.wait_recv()
 
     def part(self, p):
         return self.full[p]
 
     def drain(self):
-        for copy in self.scatter + self.gather + [self.swap]:
+        for copy in self.scatter + self.gather + self.relay + [self.swap]:
             copy.wait_send()
 
 

time: 143 us -> 139 us (0.972)
  Pallas kernels: 142 us -> 138 us
    pallas_call x1, Pallas kernels: 139 us -> 136 us  [step(): pl.pallas_call(functools.partial(kernel, sections, shards), out_shape=res...]
where the time goes in v3:
time: 139 us
  Pallas kernels  138 us (99%)
    pallas_call x1, Pallas kernels, step(): pl.pallas_call(functools.partial(kernel, sections, shards), out_shape=res...  136 us

profile of v3, /device:TPU:129, one launch (start us, length us, event | category | flops | bytes accessed | tf_op | source)
XLA Modules:
  0.0 138.9 jit_solution(3529136768743242501)
XLA Ops:
  0.6 135.8 %shard_map.84 = (bf16[2,2,448,128]{3,2,1,0:T(8,128)(2,1)}, bf16[2,2,448,128]{3,2,1,0:T(8,128)(2,1)}, bf16[1,448,512]{2,1,0:T(8,128)(2,1)}, bf16[1,448,512]{2,1,0:T(8,128)(2,1)}) custom-call(bf16[4,448,128]{2,1,0:T(8,128)(2,1)} %bitcast.8, bf16[4,2,448,128]{3,2,1,0:T(8,128)(2,1)} %bitcast.7, bf16[2,2,448,128]{3,2,1,0:T(8,128)(2,1)} %bitcast.9, ...), custom_call_target="tpu_custom_call" | custom-call | tf_op jit(solution)/shard_map/pallas_call | solution.py:501
  136.4 2.5 %shard_map.85 = (bf16[2,2,448,128]{3,2,1,0:T(8,128)(2,1)}, bf16[2,2,448,128]{3,2,1,0:T(8,128)(2,1)}, bf16[1,448,512]{2,1,0:T(8,128)(2,1)}, bf16[1,448,512]{2,1,0:T(8,128)(2,1)}) custom-call(bf16[2,2,448,128]{3,2,1,0:T(8,128)(2,1)} %get-tuple-element.12.refs_0_, bf16[2,2,448,128]{3,2,1,0:T(8,128)(2,1)} %get-tuple-element.13.refs_1_, ...), custom_call_target="tpu_custom_call" | custom-call | tf_op jit(solution)/shard_map/pallas_call | solution.py:527

commit v4 on v3

--- a/solution.py
+++ b/solution.py
@@ -33,10 +33,10 @@
     B1_GATHERED, B1_COLLECTED, F1_DONE, B1_DONE,
 ) = range(19)
 SCHEDULE = {
-    "in": (ENTERED, A0_SWAPPED, A0_SWAPPED, A0_HERE),
+    "in": (ENTERED, A0_SWAPPED, A0_SWAPPED, A0_SCATTERED),
     "kept": (ENTERED, B0_GATHERED, B0_GATHERED, B0_GATHERED),
-    "f0": (B1_COLLECTED, A1_SCATTERED, B0_DONE, B0_DONE),
-    "g0": (B1_GATHERED, B1_GATHERED, B1_SWAPPED, B0_DONE),
+    "f0": (A1_SCATTERED, B1_SWAPPED, B1_GATHERED, B0_DONE),
+    "g0": (B1_GATHERED, B1_GATHERED, B1_GATHERED, B1_GATHERED),
     "f1": (F1_DONE, F1_DONE, F1_DONE, F1_DONE),
     "g1": (B1_DONE, B1_DONE, B1_DONE, B1_DONE),
 }

time: 139 us -> 136 us (0.978)
  Pallas kernels: 138 us -> 135 us
    pallas_call x1, Pallas kernels: 136 us -> 133 us  [step(): pl.pallas_call(functools.partial(kernel, sections, shards), out_shape=res...]
where the time goes in v4:
time: 136 us
  Pallas kernels  135 us (99%)
    pallas_call x1, Pallas kernels, step(): pl.pallas_call(functools.partial(kernel, sections, shards), out_shape=res...  133 us

profile of v4, /device:TPU:129, one launch (start us, length us, event | category | flops | bytes accessed | tf_op | source)
XLA Modules:
  0.0 135.9 jit_solution(3196868805127068657)
XLA Ops:
  0.6 132.8 %shard_map.84 = (bf16[2,2,448,128]{3,2,1,0:T(8,128)(2,1)}, bf16[2,2,448,128]{3,2,1,0:T(8,128)(2,1)}, bf16[1,448,512]{2,1,0:T(8,128)(2,1)}, bf16[1,448,512]{2,1,0:T(8,128)(2,1)}) custom-call(bf16[4,448,128]{2,1,0:T(8,128)(2,1)} %bitcast.8, bf16[4,2,448,128]{3,2,1,0:T(8,128)(2,1)} %bitcast.7, bf16[2,2,448,128]{3,2,1,0:T(8,128)(2,1)} %bitcast.9, ...), custom_call_target="tpu_custom_call" | custom-call | tf_op jit(solution)/shard_map/pallas_call | solution.py:501
  133.4 2.5 %shard_map.85 = (bf16[2,2,448,128]{3,2,1,0:T(8,128)(2,1)}, bf16[2,2,448,128]{3,2,1,0:T(8,128)(2,1)}, bf16[1,448,512]{2,1,0:T(8,128)(2,1)}, bf16[1,448,512]{2,1,0:T(8,128)(2,1)}) custom-call(bf16[2,2,448,128]{3,2,1,0:T(8,128)(2,1)} %get-tuple-element.12.refs_0_, bf16[2,2,448,128]{3,2,1,0:T(8,128)(2,1)} %get-tuple-element.13.refs_1_, ...), custom_call_target="tpu_custom_call" | custom-call | tf_op jit(solution)/shard_map/pallas_call | solution.py:527
